TPU v7x, 512 devices: a whole 4x8x8 slice. The times are simulated.
512 devices in a mesh: rows: 32 (over x, y), tp: 16 (over z, core).
Axes of the slice: x: 4, y: 8, z: 8, core: 2. Of those that a mesh axis runs over, the one named last changes fastest.
Arguments:
- queries: bfloat16 [8192, 8192], P('rows', 'tp'), may hold values from -32 to 32
- nbr_keys: bfloat16 [32768, 8192], P(('rows', 'tp')), may hold values from -8 to 8
- nbr_values: bfloat16 [32768, 8192], P(('rows', 'tp')), may hold values from -15 to 15
- nbr_index: int32 [128, 2], P('rows'), may hold values from 0 to 7, all different within a row
- residual: bfloat16 [8192, 8192], P(('rows', 'tp')), may hold values from -2 to 2
- out_weight: bfloat16 [8192, 8192], P('tp', 'rows'), may hold values from -0.0625 to 0.0625
Outputs:
- mixed: bfloat16 [8192, 8192], P(('rows', 'tp'))
Inputs may be any that keep to these rules, and one draw needn't show every extreme that they name: `nbr_index`: the 2 entries of a span differ; they index the 8 neighbours retrieved for that span's own sequence shard.
All inputs are finite; a program needn't handle non-finite values.
Results may differ from a plain program's by a relative error of at most 0.022.
Values may be sent and summed in bfloat16 or wider, within the bound.
A program may use at most 64 MiB of HBM per device.

v0:
```python
import math
import jax
import jax.numpy as jnp
from jax import lax
from jax.sharding import PartitionSpec as P

HD = 128
CH = 64
R = 128


def shards(queries, nbr_keys, nbr_values, nbr_index, residual, out_weight):
    keys_local, values_local = (
        lax.all_to_all(nbr_keys, "tp", split_axis=1, concat_axis=0, tiled=True),
        lax.all_to_all(nbr_values, "tp", split_axis=1, concat_axis=0, tiled=True),
    )
    heads_local = queries.shape[1] // HD
    span_count = queries.shape[0] // CH
    neighbour_count = keys_local.shape[0] // R
    score_scale = 1.0 / math.sqrt(HD)
    query_blocks = queries.reshape(span_count, CH, heads_local, HD)
    key_blocks = keys_local.reshape(neighbour_count, R, heads_local, HD)[nbr_index]
    value_blocks = values_local.reshape(neighbour_count, R, heads_local, HD)[nbr_index]
    scores = (
        jnp.einsum(
            "cqhd,ckrhd->chqkr", query_blocks, key_blocks, preferred_element_type=jnp.float32
        )
        * score_scale
    )
    row_top = jnp.max(scores, axis=(3, 4), keepdims=True)
    weights = jnp.exp(scores - row_top)
    probs = (weights / jnp.sum(weights, axis=(3, 4), keepdims=True)).astype(jnp.bfloat16)
    attended = jnp.einsum(
        "chqkr,ckrhd->cqhd", probs, value_blocks, preferred_element_type=jnp.float32
    )
    attn = attended.astype(jnp.bfloat16).reshape(queries.shape[0], heads_local * HD)
    partial_value = jnp.dot(
        attn,
        lax.all_gather(out_weight, "rows", axis=1, tiled=True),
        preferred_element_type=jnp.float32,
    )
    summed = lax.psum_scatter(
        partial_value.astype(jnp.bfloat16), "tp", scatter_dimension=0, tiled=True
    ).astype(jnp.float32)
    return (residual.astype(jnp.float32) + summed).astype(jnp.bfloat16)


def solution(mesh):
    placed = (
        P("rows", "tp"),
        P(("rows", "tp"), None),
        P(("rows", "tp"), None),
        P("rows", None),
        P(("rows", "tp"), None),
        P("tp", "rows"),
    )
    return jax.shard_map(
        shards, mesh=mesh, in_specs=placed, out_specs=P(("rows", "tp"), None), check_vma=False
    )
```

profile of v0, /device:TPU:8, one launch (start us, length us, event | category | flops | bytes accessed | tf_op | source)
XLA Modules:
  0.0 204.7 jit_solution(4204165510992683133)
XLA Ops:
  6.5 0.0 copy-start.3
  6.5 0.0 copy-start.2
  6.5 0.0 all-gather.2.cloned.1.call-start
  6.5 0.7 all-gather.2.cloned.1.call-update
  7.3 2.3 %copy.46 = bf16[8,16,8,512]{3,2,0,1:T(8,128)(2,1)} copy(bf16[8,16,8,512]{3,2,1,0:T(8,128)(2,1)} %bitcast.35) | data formatting | bytes 2097152 | tf_op jit(solution)/shard_map/all_to_all | solution.py:14
  9.6 10.4 %all-to-all-start.1 = ((bf16[64,16,512]{2,0,1:T(8,128)(2,1)}), bf16[64,16,512]{2,0,1:T(8,128)(2,1)S(1)}, u32[]{:S(2)}, u32[]{:S(2)}) async-start(bf16[64,16,512]{2,0,1:T(8,128)(2,1)} %bitcast.29), calls=%async_computation.1 | async-start | bytes 2097152 | tf_op jit(solution)/shard_map/all_to_all | solution.py:14
  20.0 2.4 %copy.45 = bf16[8,16,8,512]{3,2,0,1:T(8,128)(2,1)} copy(bf16[8,16,8,512]{3,2,1,0:T(8,128)(2,1)} %bitcast.36) | data formatting | bytes 2097152 | tf_op jit(solution)/shard_map/all_to_all | solution.py:15
  22.4 24.3 %all-to-all-done.1 = bf16[64,16,512]{2,0,1:T(8,128)(2,1)S(1)} async-done(((bf16[64,16,512]{2,0,1:T(8,128)(2,1)}), bf16[64,16,512]{2,0,1:T(8,128)(2,1)S(1)}, u32[]{:S(2)}, u32[]{:S(2)}) %all-to-all-start.1) | async-done | bytes 1048608 | tf_op jit(solution)/shard_map/all_to_all | solution.py:14
  46.7 4.8 %all-to-all-start = ((bf16[64,16,512]{2,0,1:T(8,128)(2,1)}), bf16[64,16,512]{2,0,1:T(8,128)(2,1)S(1)}, u32[]{:S(2)}, u32[]{:S(2)}) async-start(bf16[64,16,512]{2,0,1:T(8,128)(2,1)} %bitcast.28), calls=%async_computation | async-start | bytes 2097152 | tf_op jit(solution)/shard_map/all_to_all | solution.py:15
  51.5 0.0 reduce-scatter.2.cloned.1.call-start
  51.5 0.0 copy-done.3
  51.5 0.1 copy.10
  51.6 0.1 reshape.28
  51.7 0.0 copy-done.2
  51.7 0.1 reshape.24
  51.8 0.3 reshape.23
  52.1 26.0 %all-to-all-done = bf16[64,16,512]{2,0,1:T(8,128)(2,1)S(1)} async-done(((bf16[64,16,512]{2,0,1:T(8,128)(2,1)}), bf16[64,16,512]{2,0,1:T(8,128)(2,1)S(1)}, u32[]{:S(2)}, u32[]{:S(2)}) %all-to-all-start) | async-done | bytes 1048608 | tf_op jit(solution)/shard_map/all_to_all | solution.py:15
  78.1 0.0 copy-start
  78.1 1.0 copy-done
  79.2 1.3 reshape.22
  80.5 1.4 gather_fusion.1
  82.0 1.4 gather_fusion
  83.4 0.6 fusion.11
  84.0 0.4 fusion.5
  84.4 0.5 fusion.2
  84.9 0.2 copy.17
  85.1 38.8 %all-gather.2.cloned.1.call-done = bf16[512,8192]{1,0:T(8,128)(2,1)} async-done(((bf16[512,256]{1,0:T(8,128)(2,1)}), bf16[512,8192]{1,0:T(8,128)(2,1)}) %all-gather.2.cloned.1.call-update) | async-done | bytes 8388624 | tf_op jit(solution)/shard_map/all_gather | solution.py:39
  123.9 0.0 copy-start.1
  123.9 7.7 %convolution_convert_fusion = bf16[256,8192]{1,0:T(8,128)(2,1)} fusion(bf16[512,8192]{1,0:T(8,128)(2,1)} %all-gather.2.cloned.1.call-done, bf16[32,8,4,128]{3,2,1,0:T(4,128)(2,1)S(1)} %bitcast.37), kind=kOutput, calls=%fused_computation.2 | convolution fusion | flops 2149580800 | bytes 12845056 | tf_op jit(solution)/shard_map/dot_general | solution.py:37
  131.6 0.0 reduce-scatter.2.cloned.1.call-update
  131.7 64.5 %reduce-scatter.2.cloned.1.call-done = bf16[16,8192]{1,0:T(8,128)(2,1)} async-done(((bf16[256,8192]{1,0:T(8,128)(2,1)}), bf16[16,8192]{1,0:T(8,128)(2,1)}) %reduce-scatter.2.cloned.1.call-update) | async-done | bytes 262160 | tf_op jit(solution)/shard_map/reduce_scatter | solution.py:42
  196.2 0.0 copy-done.1
  196.2 1.7 add_convert_fusion
  (2 shorter events, 0.0 us)
Async XLA Ops:
  6.5 45.0 %copy-start.3 = (s32[4,2]{0,1:T(2,128)S(1)}, s32[4,2]{0,1:T(2,128)}, u32[]{:S(2)}) copy-start(s32[4,2]{0,1:T(2,128)} %param.9) | copy-start | bytes 100
  6.5 45.2 %copy-start.2 = (bf16[256,512]{1,0:T(8,128)(2,1)S(1)}, bf16[256,512]{1,0:T(8,128)(2,1)}, u32[]{:S(2)}) copy-start(bf16[256,512]{1,0:T(8,128)(2,1)} %param.6) | copy-start | bytes 786436
  6.5 117.4 %all-gather.2.cloned.1.call-start = ((), (), s32[]{:S(2)}) async-start(), calls=%async_computation.3 | async-start | bytes 8650752 | tf_op jit(solution)/shard_map/all_gather | solution.py:39
  9.6 37.1 %all-to-all-start.1 = ((bf16[64,16,512]{2,0,1:T(8,128)(2,1)}), bf16[64,16,512]{2,0,1:T(8,128)(2,1)S(1)}, u32[]{:S(2)}, u32[]{:S(2)}) async-start(bf16[64,16,512]{2,0,1:T(8,128)(2,1)} %bitcast.29), calls=%async_computation.1 | async-start | bytes 2097152 | tf_op jit(solution)/shard_map/all_to_all | solution.py:14
  46.7 31.5 %all-to-all-start = ((bf16[64,16,512]{2,0,1:T(8,128)(2,1)}), bf16[64,16,512]{2,0,1:T(8,128)(2,1)S(1)}, u32[]{:S(2)}, u32[]{:S(2)}) async-start(bf16[64,16,512]{2,0,1:T(8,128)(2,1)} %bitcast.28), calls=%async_computation | async-start | bytes 2097152 | tf_op jit(solution)/shard_map/all_to_all | solution.py:15
  51.5 144.7 %reduce-scatter.2.cloned.1.call-start = ((), (), s32[]{:S(2)}) async-start(), calls=%async_computation.4 | async-start | bytes 4456448 | tf_op jit(solution)/shard_map/reduce_scatter | solution.py:42
  78.1 1.1 copy-start
  123.9 72.3 %copy-start.1 = (bf16[16,8192]{1,0:T(8,128)(2,1)S(1)}, bf16[16,8192]{1,0:T(8,128)(2,1)}, u32[]{:S(2)}) copy-start(bf16[16,8192]{1,0:T(8,128)(2,1)} %param.10) | copy-start | bytes 786436
Sparse Core Ops, SparseCore 0:
  10.4 113.4 all-gather.1
  131.8 64.3 reduce-scatter.1
where the time goes:
time: 205 us
  waiting for transfers between devices  154 us (75%)
  starting transfers between devices  15.3 us (7%)
  between operations  13.5 us (7%)
  local copies, waits for them, and re-layouts  10.7 us (5%)
  matrix products  8.81 us (4%)
  other arithmetic  2.14 us (1%)
    reduce_scatter x1, waiting for transfers between devices, shards(): lax.psum_scatter(partial_value.astype(jnp.bfloat16), 'tp', scatter_dimens...  64.5 us
    all_gather x1, waiting for transfers between devices, shards(): lax.all_gather(out_weight, 'rows', axis=1, tiled=True)  38.8 us
    all_to_all x1, waiting for transfers between devices, shards(): lax.all_to_all(nbr_values, 'tp', split_axis=1, concat_axis=0, tiled=True)  26 us
    all_to_all x1, waiting for transfers between devices, shards(): lax.all_to_all(nbr_keys, 'tp', split_axis=1, concat_axis=0, tiled=True)  24.3 us
    all_to_all x1, starting transfers between devices, shards(): lax.all_to_all(nbr_keys, 'tp', split_axis=1, concat_axis=0, tiled=True)  10.4 us
    dot_general x1, matrix products, shards(): jnp.dot(attn, lax.all_gather(out_weight, 'rows', axis=1, tiled=True), pre...  7.74 us
    all_to_all x1, starting transfers between devices, shards(): lax.all_to_all(nbr_values, 'tp', split_axis=1, concat_axis=0, tiled=True)  4.79 us
  transfers between devices with their start and end apart: 4, of which 4 were waited for; matrix products, arithmetic and copies ran while one was open for 5% of the time, Pallas kernels for 0%

commit v1 on v0

--- a/solution.py
+++ b/solution.py
@@ -7,6 +7,11 @@
 HD = 128
 CH = 64
 R = 128
+
+
+def gather_over(shard, axis, dim):
+    repeated = jnp.stack([shard] * lax.axis_size(axis))
+    return jnp.concatenate(lax.all_to_all(repeated, axis, 0, 0), axis=dim)
 
 
 def shards(queries, nbr_keys, nbr_values, nbr_index, residual, out_weight):
@@ -35,9 +40,7 @@
     )
     attn = attended.astype(jnp.bfloat16).reshape(queries.shape[0], heads_local * HD)
     partial_value = jnp.dot(
-        attn,
-        lax.all_gather(out_weight, "rows", axis=1, tiled=True),
-        preferred_element_type=jnp.float32,
+        attn, gather_over(out_weight, "rows", 1), preferred_element_type=jnp.float32
     )
     summed = lax.psum_scatter(
         partial_value.astype(jnp.bfloat16), "tp", scatter_dimension=0, tiled=True

time: 205 us -> 373 us (1.82)
  the two profiles are of different devices: /device:TPU:8 before, /device:TPU:2 now
where the time goes in v1:
time: 373 us
  waiting for transfers between devices  310 us (83%)
  starting transfers between devices  25.7 us (7%)
  between operations  13.5 us (4%)
  local copies, waits for them, and re-layouts  13 us (3%)
  matrix products  8.83 us (2%)
    all_to_all x1, waiting for transfers between devices, gather_over(): return jnp.concatenate(lax.all_to_all(repeated, axis, 0, 0), axis=dim)  183 us
    reduce_scatter x1, waiting for transfers between devices, shards(): lax.psum_scatter(partial_value.astype(jnp.bfloat16), 'tp', scatter_dimens...  75.6 us
    all_to_all x1, waiting for transfers between devices, shards(): lax.all_to_all(nbr_keys, 'tp', split_axis=1, concat_axis=0, tiled=True)  26.5 us
    all_to_all x1, waiting for transfers between devices, shards(): lax.all_to_all(nbr_values, 'tp', split_axis=1, concat_axis=0, tiled=True)  24.3 us
    all_to_all x1, starting transfers between devices, gather_over(): return jnp.concatenate(lax.all_to_all(repeated, axis, 0, 0), axis=dim)  10.4 us
    all_to_all x1, starting transfers between devices, shards(): lax.all_to_all(nbr_values, 'tp', split_axis=1, concat_axis=0, tiled=True)  10.4 us
    dot_general x1, matrix products, shards(): jnp.dot(attn, gather_over(out_weight, 'rows', 1), preferred_element_type=...  7.76 us
  transfers between devices with their start and end apart: 4, of which 4 were waited for; matrix products, arithmetic and copies ran while one was open for 2% of the time, Pallas kernels for 0%

profile of v1, /device:TPU:2, one launch (start us, length us, event | category | flops | bytes accessed | tf_op | source)
XLA Modules:
  0.0 372.7 jit_solution(1696617779607468065)
XLA Ops:
  6.5 0.0 copy-start.1
  6.5 2.4 copy.46
  8.9 10.4 %all-to-all-start = ((bf16[64,16,512]{2,0,1:T(8,128)(2,1)}), bf16[64,16,512]{2,0,1:T(8,128)(2,1)S(1)}, u32[]{:S(2)}, u32[]{:S(2)}) async-start(bf16[64,16,512]{2,0,1:T(8,128)(2,1)} %bitcast.31), calls=%async_computation | async-start | bytes 2097152 | tf_op jit(solution)/shard_map/all_to_all | solution.py:20
  19.3 2.4 copy.47
  21.7 24.3 %all-to-all-done = bf16[64,16,512]{2,0,1:T(8,128)(2,1)S(1)} async-done(((bf16[64,16,512]{2,0,1:T(8,128)(2,1)}), bf16[64,16,512]{2,0,1:T(8,128)(2,1)S(1)}, u32[]{:S(2)}, u32[]{:S(2)}) %all-to-all-start) | async-done | bytes 1048608 | tf_op jit(solution)/shard_map/all_to_all | solution.py:20
  46.0 4.8 %all-to-all-start.1 = ((bf16[64,16,512]{2,0,1:T(8,128)(2,1)}), bf16[64,16,512]{2,0,1:T(8,128)(2,1)S(1)}, u32[]{:S(2)}, u32[]{:S(2)}) async-start(bf16[64,16,512]{2,0,1:T(8,128)(2,1)} %bitcast.32), calls=%async_computation.1 | async-start | bytes 2097152 | tf_op jit(solution)/shard_map/all_to_all | solution.py:19
  50.8 0.0 copy-done.1
  50.8 0.1 copy.18
  50.9 26.5 %all-to-all-done.1 = bf16[64,16,512]{2,0,1:T(8,128)(2,1)S(1)} async-done(((bf16[64,16,512]{2,0,1:T(8,128)(2,1)}), bf16[64,16,512]{2,0,1:T(8,128)(2,1)S(1)}, u32[]{:S(2)}, u32[]{:S(2)}) %all-to-all-start.1) | async-done | bytes 1048608 | tf_op jit(solution)/shard_map/all_to_all | solution.py:19
  77.4 4.2 %stack.2 = bf16[32,512,256]{1,2,0:T(8,128)(2,1)} broadcast(bf16[512,256]{0,1:T(8,128)(2,1)S(1)} %copy.18), dimensions={1,2} | broadcast | bytes 8650752 | tf_op jit(solution)/shard_map/stack | solution.py:13
  81.6 0.0 copy-start.3
  81.6 0.0 copy-start.2
  81.6 10.4 %all-to-all-start.2 = ((bf16[32,512,256]{1,2,0:T(8,128)(2,1)}), bf16[32,512,256]{1,2,0:T(8,128)(2,1)}, u32[]{:S(2)}, u32[]{:S(2)}) async-start(bf16[32,512,256]{1,2,0:T(8,128)(2,1)} %stack.2), calls=%async_computation.2 | async-start | bytes 16777216 | tf_op jit(solution)/shard_map/all_to_all | solution.py:14
  92.1 0.0 reduce-scatter.2.cloned.1.call-start
  92.1 0.0 copy-done.3
  92.1 0.1 copy.10
  92.2 0.1 reshape.38
  92.3 0.0 copy-done.2
  92.3 0.1 reshape.32
  92.4 0.3 reshape.30
  92.7 0.3 reshape.31
  93.0 1.4 gather_fusion
  94.4 1.4 gather_fusion.1
  95.9 0.6 fusion.11
  96.5 0.4 fusion.5
  96.9 0.5 fusion.2
  97.4 0.2 copy.17
  97.6 183.2 %all-to-all-done.2 = bf16[32,512,256]{1,2,0:T(8,128)(2,1)} async-done(((bf16[32,512,256]{1,2,0:T(8,128)(2,1)}), bf16[32,512,256]{1,2,0:T(8,128)(2,1)}, u32[]{:S(2)}, u32[]{:S(2)}) %all-to-all-start.2) | async-done | bytes 8388640 | tf_op jit(solution)/shard_map/all_to_all | solution.py:14
  280.8 0.0 copy-start
  280.8 7.8 %convolution_convert_fusion = bf16[256,8192]{1,0:T(8,128)(2,1)} fusion(bf16[512,8192]{0,1:T(8,128)(2,1)} %bitcast.10, bf16[32,8,4,128]{3,2,1,0:T(4,128)(2,1)S(1)} %bitcast.38), kind=kOutput, calls=%fused_computation.2 | convolution fusion | flops 2149580800 | bytes 12845056 | tf_op jit(solution)/shard_map/dot_general | solution.py:42
  288.5 0.0 reduce-scatter.2.cloned.1.call-update
  288.5 75.6 %reduce-scatter.2.cloned.1.call-done = bf16[16,8192]{1,0:T(8,128)(2,1)} async-done(((bf16[256,8192]{1,0:T(8,128)(2,1)}), bf16[16,8192]{1,0:T(8,128)(2,1)}) %reduce-scatter.2.cloned.1.call-update) | async-done | bytes 262160 | tf_op jit(solution)/shard_map/reduce_scatter | solution.py:45
  364.2 0.0 copy-done
  364.2 1.7 add_convert_fusion
  (2 shorter events, 0.0 us)
Async XLA Ops:
  6.5 44.2 %copy-start.1 = (bf16[512,256]{1,0:T(8,128)(2,1)S(1)}, bf16[512,256]{1,0:T(8,128)(2,1)}, u32[]{:S(2)}) copy-start(bf16[512,256]{1,0:T(8,128)(2,1)} %param.11) | copy-start | bytes 786436
  8.9 37.1 %all-to-all-start = ((bf16[64,16,512]{2,0,1:T(8,128)(2,1)}), bf16[64,16,512]{2,0,1:T(8,128)(2,1)S(1)}, u32[]{:S(2)}, u32[]{:S(2)}) async-start(bf16[64,16,512]{2,0,1:T(8,128)(2,1)} %bitcast.31), calls=%async_computation | async-start | bytes 2097152 | tf_op jit(solution)/shard_map/all_to_all | solution.py:20
  46.0 31.5 %all-to-all-start.1 = ((bf16[64,16,512]{2,0,1:T(8,128)(2,1)}), bf16[64,16,512]{2,0,1:T(8,128)(2,1)S(1)}, u32[]{:S(2)}, u32[]{:S(2)}) async-start(bf16[64,16,512]{2,0,1:T(8,128)(2,1)} %bitcast.32), calls=%async_computation.1 | async-start | bytes 2097152 | tf_op jit(solution)/shard_map/all_to_all | solution.py:19
  81.6 10.5 %copy-start.3 = (s32[4,2]{0,1:T(2,128)S(1)}, s32[4,2]{0,1:T(2,128)}, u32[]{:S(2)}) copy-start(s32[4,2]{0,1:T(2,128)} %param.9) | copy-start | bytes 100
  81.6 10.7 %copy-start.2 = (bf16[256,512]{1,0:T(8,128)(2,1)S(1)}, bf16[256,512]{1,0:T(8,128)(2,1)}, u32[]{:S(2)}) copy-start(bf16[256,512]{1,0:T(8,128)(2,1)} %param.6) | copy-start | bytes 786436
  81.6 199.1 %all-to-all-start.2 = ((bf16[32,512,256]{1,2,0:T(8,128)(2,1)}), bf16[32,512,256]{1,2,0:T(8,128)(2,1)}, u32[]{:S(2)}, u32[]{:S(2)}) async-start(bf16[32,512,256]{1,2,0:T(8,128)(2,1)} %stack.2), calls=%async_computation.2 | async-start | bytes 16777216 | tf_op jit(solution)/shard_map/all_to_all | solution.py:14
  92.1 272.1 %reduce-scatter.2.cloned.1.call-start = ((), (), s32[]{:S(2)}) async-start(), calls=%async_computation.4 | async-start | bytes 4456448 | tf_op jit(solution)/shard_map/reduce_scatter | solution.py:45
  280.8 83.4 %copy-start = (bf16[16,8192]{1,0:T(8,128)(2,1)S(1)}, bf16[16,8192]{1,0:T(8,128)(2,1)}, u32[]{:S(2)}) copy-start(bf16[16,8192]{1,0:T(8,128)(2,1)} %param.10) | copy-start | bytes 786436
Sparse Core Ops, SparseCore 0:
  288.7 75.4 reduce-scatter.1
